TPU v7x, 32 devices: a whole 2x2x4 slice. The times are simulated.
32 devices in a mesh: grp: 2 (over y), blk: 16 (over z, x, core).
Axes of the slice: x: 2, y: 2, z: 4, core: 2. Of those that a mesh axis runs over, the one named last changes fastest.
Arguments:
- amplitudes: bfloat16 [32, 640, 640], P('grp', 'blk'), parts along dimension 0, may hold values from -0.009765625 to 0.009765625
- factors: bfloat16 [16, 640, 2560], P('blk'), may hold values from -0.875 to 0.875
Outputs:
- residual: float32 [16, 3, 32], P('blk', None, 'grp'), parts along dimension 2
There are 2 independent parts, one for each index of `grp`. A program takes and returns all parts, laid end to end along the dimension named above; an argument that names none is the same for every part. Nothing has to cross between parts.
All inputs are finite; a program needn't handle non-finite values.
Results may differ from a plain program's by a relative error of at most 0.003.
Values may be sent and summed in bfloat16 or wider, within the bound.
A program may use at most 64 MiB of HBM per device.

v0:
```python
import functools

import jax
import jax.numpy as jnp
from jax import lax
from jax.experimental import pallas as pl
from jax.experimental.pallas import tpu as pltpu
from jax.sharding import PartitionSpec as P

MESH = pl.DeviceIdType.MESH
CHUNKS = 4
NT = (((1,), (1,)), ((), ()))


def kernel(
    n,
    t_hbm,
    f_hbm,
    out_ref,
    own,
    near,
    amps,
    cast_off,
    both,
    made,
    got,
    part,
    back,
    local_sem,
    near_send,
    near_recv,
    relay_send,
    amp_sem,
    made_send,
    got_recv,
    part_send,
    back_recv,
):
    g = lax.axis_index("grp")
    m = lax.axis_index("blk")
    other = 1 - g
    behind = lax.rem(m + n - 1, n)
    odd = lax.rem(m, 2)
    pairs, rows, wide = t_hbm.shape
    half = wide // 2
    span = half // CHUNKS

    copy_f = pltpu.make_async_copy(f_hbm, own, local_sem.at[0])
    copy_t = pltpu.make_async_copy(t_hbm, amps, local_sem.at[1])
    copy_f.start()
    copy_t.start()

    barrier = pltpu.get_barrier_semaphore()

    @pl.loop(1, n)
    def _(s):
        pl.semaphore_signal(barrier, inc=1, device_id=(g, lax.rem(m + s, n)), device_id_type=MESH)

    @pl.loop(0, n)
    def _(s):
        pl.semaphore_signal(barrier, inc=1, device_id=(other, lax.rem(m + s, n)), device_id_type=MESH)

    pl.semaphore_wait(barrier, 2 * n - 1)

    def near_copy(h, q):
        return pltpu.make_async_remote_copy(
            src_ref=f_hbm.at[h, pl.ds(q * span, span)],
            dst_ref=near.at[h, pl.ds(q * span, span)],
            send_sem=near_send.at[h, q],
            recv_sem=near_recv.at[h, q],
            device_id=(g, behind),
            device_id_type=MESH,
        )

    def relay_copy(q):
        return pltpu.make_async_remote_copy(
            src_ref=near.at[g, pl.ds(q * span, span)],
            dst_ref=near.at[g, pl.ds(q * span, span)],
            send_sem=relay_send.at[q],
            recv_sem=near_recv.at[g, q],
            device_id=(other, m),
            device_id_type=MESH,
        )

    for q in range(CHUNKS):
        near_copy(g, q).start()

    @pl.when(odd == 1)
    def _():
        for q in range(CHUNKS):
            near_copy(other, q).start()

    copy_t.wait()
    left = amps[:, :, :half]
    right = amps[:, :, half:]
    low = g == 0
    both[g] = jnp.where(low, left, right)
    cast_off[...] = jnp.where(low, right, left)
    amp_copy = pltpu.make_async_remote_copy(
        src_ref=cast_off,
        dst_ref=both.at[g],
        send_sem=amp_sem.at[0],
        recv_sem=amp_sem.at[1],
        device_id=(other, m),
        device_id_type=MESH,
    )
    amp_copy.start()

    blocks = n // 2

    def product(k, left_ref, h, right_ref):
        tile = lax.dot_general(
            left_ref[h], right_ref[g], NT, preferred_element_type=jnp.float32
        )
        for b in range(blocks):
            made[k, h * blocks + b] = tile[b * rows : (b + 1) * rows].astype(jnp.bfloat16)

    def made_copy(k, s):
        to = lax.rem(m + n - s, n)
        return pltpu.make_async_remote_copy(
            src_ref=made.at[k, to],
            dst_ref=got.at[k, s],
            send_sem=made_send.at[k, s],
            recv_sem=got_recv.at[k, s],
            device_id=(g, to),
            device_id_type=MESH,
        )

    def send(k):
        @pl.loop(1, n)
        def _(s):
            made_copy(k, s).start()

        got[k, 0] = made[k, m]

    copy_f.wait()
    for h in range(2):
        product(0, own, h, own)
    send(0)

    for q in range(CHUNKS):
        near_copy(g, q).wait_recv()

        @pl.when(odd == 1)
        def _():
            relay_copy(q).start()

    for h in range(2):
        product(1, own, h, near)
    send(1)
    product(2, near, g, own)
    for q in range(CHUNKS):
        near_copy(other, q).wait_recv()
    product(2, near, other, own)
    send(2)

    amp_copy.wait_recv()
    flat = both[...].astype(jnp.float32).reshape(2 * pairs * rows, half).astype(jnp.bfloat16)
    columns = 2 * pairs * rows
    on_diagonal = lax.broadcasted_iota(jnp.int32, (rows, columns), 0) == lax.rem(
        lax.broadcasted_iota(jnp.int32, (rows, columns), 1), rows
    )
    lane = lax.broadcasted_iota(jnp.int32, (columns, 128), 0)
    first = lax.broadcasted_iota(jnp.int32, (columns, 128), 1) * rows
    chooser = jnp.where((lane >= first) & (lane < first + rows), 1.0, 0.0)
    part[...] = jnp.zeros_like(part)
    for k in range(3):

        @pl.loop(1, n)
        def _(s):
            made_copy(k, s).wait_recv()

        tiles = got[k].astype(jnp.float32).reshape(n * rows, half).astype(jnp.bfloat16)
        grid = lax.dot_general(tiles, flat, NT, preferred_element_type=jnp.float32)
        grid = jnp.where(on_diagonal[None], grid.reshape(n, rows, columns), 0.0)
        sums = jnp.dot(
            jnp.sum(grid, axis=1),
            chooser,
            preferred_element_type=jnp.float32,
            precision=lax.Precision.HIGHEST,
        )
        for s in range(n):
            part[s, k : k + 1] = sums[s : s + 1]

    def part_copy(plane, s):
        return pltpu.make_async_remote_copy(
            src_ref=part.at[s],
            dst_ref=back.at[g, s],
            send_sem=part_send.at[plane, s],
            recv_sem=back_recv.at[g, s],
            device_id=(plane, lax.rem(m + s, n)),
            device_id_type=MESH,
        )

    def back_wait(plane, s):
        return pltpu.make_async_remote_copy(
            src_ref=part.at[s],
            dst_ref=back.at[plane, s],
            send_sem=part_send.at[plane, s],
            recv_sem=back_recv.at[plane, s],
            device_id=(plane, lax.rem(m + n - s, n)),
            device_id_type=MESH,
        )

    @pl.loop(0, n)
    def _(s):
        part_copy(other, s).start()

    @pl.loop(1, n)
    def _(s):
        part_copy(g, s).start()

    back[g, 0] = part[0]

    @pl.loop(1, n)
    def _(s):
        back_wait(g, s).wait_recv()

    @pl.loop(0, n)
    def _(s):
        back_wait(other, s).wait_recv()

    total = jnp.sum(back[...].reshape(2 * n, 8, 128), axis=0)
    out_ref[0] = jnp.where(low, total[:3, :pairs], total[:3, pairs : 2 * pairs])

    for q in range(CHUNKS):
        near_copy(g, q).wait_send()

    @pl.when(odd == 1)
    def _():
        for q in range(CHUNKS):
            near_copy(other, q).wait_send()
            relay_copy(q).wait_send()

    amp_copy.wait_send()
    for k in range(3):

        @pl.loop(1, n)
        def _(s):
            made_copy(k, s).wait_send()

    @pl.loop(0, n)
    def _(s):
        part_copy(other, s).wait_send()

    @pl.loop(1, n)
    def _(s):
        part_copy(g, s).wait_send()


def fused(n, amplitudes, factors):
    pairs, rows, wide = amplitudes.shape
    deep = factors.shape[2]
    half = wide // 2
    dma = pltpu.SemaphoreType.DMA
    bf16 = jnp.bfloat16
    return pl.pallas_call(
        functools.partial(kernel, n),
        out_shape=jax.ShapeDtypeStruct((1, 3, pairs), jnp.float32),
        in_specs=[pl.BlockSpec(memory_space=pl.ANY)] * 2,
        out_specs=pl.BlockSpec(memory_space=pltpu.VMEM),
        scratch_shapes=[
            pltpu.VMEM((2, half, deep), bf16),
            pltpu.VMEM((2, half, deep), bf16),
            pltpu.VMEM((pairs, rows, wide), bf16),
            pltpu.VMEM((pairs, rows, half), bf16),
            pltpu.VMEM((2, pairs, rows, half), bf16),
            pltpu.VMEM((3, n, rows, half), bf16),
            pltpu.VMEM((3, n, rows, half), bf16),
            pltpu.VMEM((n, 8, 128), jnp.float32),
            pltpu.VMEM((2, n, 8, 128), jnp.float32),
            dma((2,)),
            dma((2, CHUNKS)),
            dma((2, CHUNKS)),
            dma((CHUNKS,)),
            dma((2,)),
            dma((3, n)),
            dma((3, n)),
            dma((2, n)),
            dma((2, n)),
        ],
        compiler_params=pltpu.CompilerParams(
            collective_id=0, has_side_effects=True, vmem_limit_bytes=48 * 2**20
        ),
    )(amplitudes, factors.reshape(2, half, deep))


def product_rows(left, right):
    return lax.dot_general(left, right, NT, preferred_element_type=jnp.float32).astype(jnp.bfloat16)


def gathered(n, amplitudes, factors):
    own = factors[0]
    near = lax.ppermute(factors, "blk", [(i, (i + n - 1) % n) for i in range(n)])[0]
    block = lax.all_gather(amplitudes, "blk", axis=1, tiled=True)
    cross = product_rows(own, near)
    tiles = jnp.stack([product_rows(own, own), cross, cross.T])
    total = jnp.einsum("pcd,kcd->kp", block, tiles, preferred_element_type=jnp.float32)
    return total[None]


def solution(mesh):
    n = mesh.shape["blk"]

    def body(amplitudes, factors):
        whole = amplitudes.shape[1] % 8 == 0 and n % 2 == 0 and mesh.shape["grp"] == 2
        return (fused if whole else gathered)(n, amplitudes, factors)

    return jax.shard_map(
        body,
        mesh=mesh,
        in_specs=(P("grp", "blk", None), P("blk", None, None)),
        out_specs=P("blk", None, "grp"),
        check_vma=False,
    )
```

profile of v0, /device:TPU:0, one launch (start us, length us, event | category | flops | bytes accessed | tf_op | source)
XLA Modules:
  0.0 71.2 jit_solution(17041836380028938713)
XLA Ops:
  0.0 0.0 copy-start
  0.0 1.9 %copy-done = bf16[1,640,2560]{2,1,0:T(8,128)(2,1)S(1)} copy-done((bf16[1,640,2560]{2,1,0:T(8,128)(2,1)S(1)}, bf16[1,640,2560]{2,1,0:T(8,128)(2,1)}, u32[]{:S(2)}) %copy-start) | copy-done | bytes 3276824
  1.9 0.0 copy-start.1
  1.9 1.1 %copy-done.1 = bf16[16,40,640]{2,1,0:T(8,128)(2,1)S(1)} copy-done((bf16[16,40,640]{2,1,0:T(8,128)(2,1)S(1)}, bf16[16,40,640]{2,1,0:T(8,128)(2,1)}, u32[]{:S(2)}) %copy-start.1) | copy-done | bytes 819224
  3.1 67.5 %shard_map.28 = f32[1,3,16]{2,1,0:T(4,128)S(1)} custom-call(bf16[16,40,640]{2,1,0:T(8,128)(2,1)S(1)} %copy-done.1, bf16[2,320,2560]{2,1,0:T(8,128)(2,1)S(1)} %bitcast.1), custom_call_target="tpu_custom_call" | custom-call | tf_op jit(solution)/shard_map/pallas_call | solution.py:257
  70.6 0.6 copy.3
Async XLA Ops:
  0.0 1.9 %copy-start = (bf16[1,640,2560]{2,1,0:T(8,128)(2,1)S(1)}, bf16[1,640,2560]{2,1,0:T(8,128)(2,1)}, u32[]{:S(2)}) copy-start(bf16[1,640,2560]{2,1,0:T(8,128)(2,1)} %param.3) | copy-start | bytes 9830404
  1.9 1.1 %copy-start.1 = (bf16[16,40,640]{2,1,0:T(8,128)(2,1)S(1)}, bf16[16,40,640]{2,1,0:T(8,128)(2,1)}, u32[]{:S(2)}) copy-start(bf16[16,40,640]{2,1,0:T(8,128)(2,1)} %t_hbm.1) | copy-start | bytes 2457604
where the time goes:
time: 71.4 us; the launch traced here: 71.2 us
  Pallas kernels  67.5 us (95%)
  local copies, waits for them, and re-layouts  3.63 us (5%)
    pallas_call x1, Pallas kernels, fused(): pl.pallas_call(functools.partial(kernel, n), out_shape=jax.ShapeDtypeStru...  67.5 us
    unnamed x4, local copies, waits for them, and re-layouts  3.07 us

commit v1 on v0

--- a/solution.py
+++ b/solution.py
@@ -8,7 +8,7 @@
 from jax.sharding import PartitionSpec as P
 
 MESH = pl.DeviceIdType.MESH
-CHUNKS = 4
+CHUNKS = 2
 NT = (((1,), (1,)), ((), ()))
 
 
@@ -280,7 +280,7 @@
             dma((2, n)),
         ],
         compiler_params=pltpu.CompilerParams(
-            collective_id=0, has_side_effects=True, vmem_limit_bytes=48 * 2**20
+            collective_id=0, has_side_effects=True, vmem_limit_bytes=61 * 2**20
         ),
     )(amplitudes, factors.reshape(2, half, deep))
 

time: 71.4 us -> 69.1 us (0.968)
  local copies, waits for them, and re-layouts: 3.63 us -> 1.25 us
    unnamed x4 -> x0, local copies, waits for them, and re-layouts: 3.07 us -> none
where the time goes in v1:
time: 69.1 us; the launch traced here: 69 us
  Pallas kernels  67.7 us (98%)
  local copies, waits for them, and re-layouts  1.25 us (2%)
    pallas_call x1, Pallas kernels, fused(): pl.pallas_call(functools.partial(kernel, n), out_shape=jax.ShapeDtypeStru...  67.7 us

profile of v1, /device:TPU:0, one launch (start us, length us, event | category | flops | bytes accessed | tf_op | source)
XLA Modules:
  0.0 69.0 jit_solution(10788248387305086902)
XLA Ops:
  0.0 67.7 %shard_map.28 = f32[1,3,16]{2,1,0:T(4,128)} custom-call(bf16[16,40,640]{2,1,0:T(8,128)(2,1)} %t_hbm.1, bf16[2,320,2560]{2,1,0:T(8,128)(2,1)} %bitcast.1), custom_call_target="tpu_custom_call" | custom-call | tf_op jit(solution)/shard_map/pallas_call | solution.py:257
  67.7 1.2 %copy.3 = f32[1,3,16]{2,0,1:T(1,128)} copy(f32[1,3,16]{2,1,0:T(4,128)} %shard_map.28) | data formatting | bytes 384 | tf_op jit(solution)/shard_map/pallas_call | solution.py:257

commit v2 on v1

--- a/solution.py
+++ b/solution.py
@@ -60,42 +60,56 @@
     def _(s):
         pl.semaphore_signal(barrier, inc=1, device_id=(other, lax.rem(m + s, n)), device_id_type=MESH)
 
-    pl.semaphore_wait(barrier, 2 * n - 1)
-
-    def near_copy(h, q):
-        return pltpu.make_async_remote_copy(
-            src_ref=f_hbm.at[h, pl.ds(q * span, span)],
-            dst_ref=near.at[h, pl.ds(q * span, span)],
-            send_sem=near_send.at[h, q],
-            recv_sem=near_recv.at[h, q],
-            device_id=(g, behind),
-            device_id_type=MESH,
-        )
-
-    def relay_copy(q):
-        return pltpu.make_async_remote_copy(
-            src_ref=near.at[g, pl.ds(q * span, span)],
-            dst_ref=near.at[g, pl.ds(q * span, span)],
-            send_sem=relay_send.at[q],
-            recv_sem=near_recv.at[g, q],
-            device_id=(other, m),
-            device_id_type=MESH,
-        )
-
-    for q in range(CHUNKS):
-        near_copy(g, q).start()
-
-    @pl.when(odd == 1)
-    def _():
-        for q in range(CHUNKS):
-            near_copy(other, q).start()
-
     copy_t.wait()
     left = amps[:, :, :half]
     right = amps[:, :, half:]
     low = g == 0
     both[g] = jnp.where(low, left, right)
     cast_off[...] = jnp.where(low, right, left)
+
+    blocks = n // 2
+
+    def product(k, left_ref, h, right_ref):
+        tile = lax.dot_general(
+            left_ref[h], right_ref[g], NT, preferred_element_type=jnp.float32
+        )
+        for b in range(blocks):
+            made[k, h * blocks + b] = tile[b * rows : (b + 1) * rows].astype(jnp.bfloat16)
+
+    copy_f.wait()
+    for h in range(2):
+        product(0, own, h, own)
+
+    pl.semaphore_wait(barrier, 2 * n - 1)
+
+    def near_copy(h, q):
+        return pltpu.make_async_remote_copy(
+            src_ref=f_hbm.at[h, pl.ds(q * span, span)],
+            dst_ref=near.at[h, pl.ds(q * span, span)],
+            send_sem=near_send.at[h, q],
+            recv_sem=near_recv.at[h, q],
+            device_id=(g, behind),
+            device_id_type=MESH,
+        )
+
+    def relay_copy(q):
+        return pltpu.make_async_remote_copy(
+            src_ref=near.at[g, pl.ds(q * span, span)],
+            dst_ref=near.at[g, pl.ds(q * span, span)],
+            send_sem=relay_send.at[q],
+            recv_sem=near_recv.at[g, q],
+            device_id=(other, m),
+            device_id_type=MESH,
+        )
+
+    for q in range(CHUNKS):
+        near_copy(g, q).start()
+
+    @pl.when(odd == 1)
+    def _():
+        for q in range(CHUNKS):
+            near_copy(other, q).start()
+
     amp_copy = pltpu.make_async_remote_copy(
         src_ref=cast_off,
         dst_ref=both.at[g],
@@ -106,15 +120,6 @@
     )
     amp_copy.start()
 
-    blocks = n // 2
-
-    def product(k, left_ref, h, right_ref):
-        tile = lax.dot_general(
-            left_ref[h], right_ref[g], NT, preferred_element_type=jnp.float32
-        )
-        for b in range(blocks):
-            made[k, h * blocks + b] = tile[b * rows : (b + 1) * rows].astype(jnp.bfloat16)
-
     def made_copy(k, s):
         to = lax.rem(m + n - s, n)
         return pltpu.make_async_remote_copy(
@@ -133,9 +138,6 @@
 
         got[k, 0] = made[k, m]
 
-    copy_f.wait()
-    for h in range(2):
-        product(0, own, h, own)
     send(0)
 
     for q in range(CHUNKS):
@@ -147,6 +149,8 @@
 
     for h in range(2):
         product(1, own, h, near)
+    for q in range(CHUNKS):
+        near_copy(g, q).wait_send()
     send(1)
     product(2, near, g, own)
     for q in range(CHUNKS):
@@ -222,9 +226,6 @@
 
     total = jnp.sum(back[...].reshape(2 * n, 8, 128), axis=0)
     out_ref[0] = jnp.where(low, total[:3, :pairs], total[:3, pairs : 2 * pairs])
-
-    for q in range(CHUNKS):
-        near_copy(g, q).wait_send()
 
     @pl.when(odd == 1)
     def _():

time: 69.1 us -> 67.7 us (0.980)
  Pallas kernels: 67.7 us -> 66.3 us
    pallas_call x1, Pallas kernels: 67.7 us -> 66.3 us  [fused(): pl.pallas_call(functools.partial(kernel, n), out_shape=jax.ShapeDtypeStru...]
where the time goes in v2:
time: 67.7 us; the launch traced here: 67.5 us
  Pallas kernels  66.3 us (98%)
  local copies, waits for them, and re-layouts  1.25 us (2%)
    pallas_call x1, Pallas kernels, fused(): pl.pallas_call(functools.partial(kernel, n), out_shape=jax.ShapeDtypeStru...  66.3 us

profile of v2, /device:TPU:0, one launch (start us, length us, event | category | flops | bytes accessed | tf_op | source)
XLA Modules:
  0.0 67.5 jit_solution(4987081356447481853)
XLA Ops:
  0.0 66.3 %shard_map.28 = f32[1,3,16]{2,1,0:T(4,128)} custom-call(bf16[16,40,640]{2,1,0:T(8,128)(2,1)} %t_hbm.1, bf16[2,320,2560]{2,1,0:T(8,128)(2,1)} %bitcast.1), custom_call_target="tpu_custom_call" | custom-call | tf_op jit(solution)/shard_map/pallas_call | solution.py:258
  66.3 1.2 %copy.3 = f32[1,3,16]{2,0,1:T(1,128)} copy(f32[1,3,16]{2,1,0:T(4,128)} %shard_map.28) | data formatting | bytes 384 | tf_op jit(solution)/shard_map/pallas_call | solution.py:258
